TPU v7x, 32 devices: a whole 2x2x4 slice. The times are simulated.
32 devices in a mesh: comp: 2 (over x), lon: 8 (over z, core), ch: 2 (over y).
Axes of the slice: x: 2, y: 2, z: 4, core: 2. Of those that a mesh axis runs over, the one named last changes fastest.
Arguments:
- ocean_state: bfloat16 [3, 128, 64, 256], P(None, 'ch', ('comp', 'lon')), may hold values from -6 to 6
- ocean_mask: int32 [64, 256], P(('comp', 'lon')), may hold values 0 or 1
- air_state: bfloat16 [2, 192, 32, 2, 256], P(None, 'ch', 'lon', None, 'comp'), may hold values from -6 to 6
- surface_temp: float32 [64, 256], P(('comp', 'lon')), may hold values from -6 to 6
- air_fluxes: float32 [4, 32, 2, 256], P(None, 'lon', None, 'comp'), may hold values from -6 to 6
- ocean_kernel: float32 [128, 3, 7, 7], P('ch'), may hold values from -0.5 to 0.5
- ocean_gain: float32 [128], replicated, may hold values from 0.5 to 1.5
- ocean_up: bfloat16 [128, 512], replicated, may hold values from -0.5 to 0.5
- ocean_down: bfloat16 [512, 128], replicated, may hold values from -0.25 to 0.25
- air_kernel: float32 [192, 3, 7, 7], P('ch'), may hold values from -0.5 to 0.5
- air_gain: float32 [192], replicated, may hold values from 0.5 to 1.5
- air_up: bfloat16 [192, 768], replicated, may hold values from -0.4375 to 0.4375
- air_down: bfloat16 [768, 192], replicated, may hold values from -0.21875 to 0.21875
- flux_weight: float32 [4, 128], P(None, 'ch'), may hold values from -3 to 3
- temp_weight: float32 [192], P('ch'), may hold values from -1 to 1
Outputs:
- ocean_next: bfloat16 [3, 128, 64, 256], P(None, 'ch', ('comp', 'lon'))
- air_next: bfloat16 [2, 192, 32, 2, 256], P(None, 'ch', 'lon', None, 'comp')
All inputs are finite; a program needn't handle non-finite values. No bound on the sum of `ocean_mask` on one device may be relied on, other than what follows from the above.
Results may differ from a plain program's by a relative error of at most 0.007.
Values may be sent and summed in bfloat16 or wider, within the bound.
A program may use at most 64 MiB of HBM per device.

v0:
```python
import functools

import jax
import jax.numpy as jnp
from jax import lax
from jax.experimental import pallas as pl
from jax.experimental.pallas import tpu as pltpu
from jax.sharding import PartitionSpec as P

LANES = 128
ROWS = 16
HALF = 8
RIM = 3
TAPS = 147
MESH = pl.DeviceIdType.MESH
F32, BF16 = jnp.float32, jnp.bfloat16


def tap_sum(values, wb, group, d, levels, width):
    sums = [None] * levels
    for a in range(3):
        for b in range(7):
            w = wb[group, a * 49 + b * 7 + d][None]
            for lev in range(levels):
                src = lev + a - 1
                if 0 <= src < levels:
                    term = w * values(src, b)
                    sums[lev] = term if sums[lev] is None else sums[lev] + term
    return sums


def ocean_group(main, wb, total, rows, group, levels, tiles, width):
    lane = lax.broadcasted_iota(jnp.int32, (width, HALF, LANES), 2)
    zero = jnp.zeros((width, HALF, LANES), F32)
    for step, d in enumerate((3, 0, 1, 2, 4, 5, 6)):
        s = d - 3
        sums = [
            tap_sum(lambda lev, b: main[lev, p, b : b + width, rows, :], wb, group, d, levels, width)
            for p in range(tiles)
        ]
        for p in range(tiles):
            for lev in range(levels):
                v = sums[p][lev]
                if s > 0:
                    beside = sums[p + 1][lev] if p + 1 < tiles else zero
                    v = pltpu.roll(jnp.where(lane < s, beside, v), LANES - s, 2)
                elif s < 0:
                    beside = sums[p - 1][lev] if p > 0 else zero
                    v = pltpu.roll(jnp.where(lane >= LANES + s, beside, v), -s, 2)
                if step == 0:
                    total[lev, p, :, rows, :] = v
                else:
                    total[lev, p, :, rows, :] += v


def air_group(main, wrap, wb, total, rows, group, levels, halves, width):
    lane = lax.broadcasted_iota(jnp.int32, (width + 2 * RIM, HALF, LANES), 2)
    for p in range(halves):
        for step, d in enumerate((3, 0, 1, 2, 4, 5, 6)):
            s = d - 3
            shifted = []
            for lev in range(levels):
                v = main[lev, p, :, rows, :]
                if s > 0:
                    v = pltpu.roll(jnp.where(lane < s, wrap[lev, p], v), LANES - s, 2)
                elif s < 0:
                    v = pltpu.roll(jnp.where(lane >= LANES + s, wrap[lev, p], v), -s, 2)
                shifted.append(v)
            sums = tap_sum(lambda lev, b: shifted[lev][b : b + width], wb, group, d, levels, width)
            for lev in range(levels):
                if step == 0:
                    total[lev, p, :, rows, :] = sums[lev]
                else:
                    total[lev, p, :, rows, :] += sums[lev]


def spread_taps(k_ref, stack, turned, wb):
    ch = k_ref.shape[3]
    for a in range(3):
        for b in range(7):
            at = (a * 7 + b) * HALF
            stack[at : at + 7, 0:ch] = k_ref[a, b]
    for half in range(2):
        turned[half] = jnp.transpose(stack[half * LANES : (half + 1) * LANES, :])

    def body(group, carry):
        rows = pl.ds(pl.multiple_of(group * HALF, HALF), HALF)
        taps = [turned[half, rows, :] for half in range(2)]
        for tap in range(TAPS):
            half, at = divmod(tap // 7 * HALF + tap % 7, LANES)
            wb[group, tap] = jnp.broadcast_to(taps[half][:, at : at + 1], (HALF, LANES))
        return carry

    lax.fori_loop(0, wb.shape[0], body, 0)


def gelu(v):
    scale = (2.0 / jnp.pi) ** 0.5
    half = 0.5 * v
    return half + half * jnp.tanh(v * (scale + (scale * 0.044715) * (v * v)))


def mlp(mine, other, resid, gain, up, down):
    values = jnp.concatenate([mine, other], axis=0).astype(F32)
    center = jnp.mean(values, axis=0, keepdims=True)
    moved = values - center
    spread = jnp.mean(moved * moved, axis=0, keepdims=True)
    normed = (moved * lax.rsqrt(spread + 1e-06) * gain).astype(BF16)
    hidden = gelu(jnp.dot(up, normed, preferred_element_type=F32)).astype(BF16)
    update = jnp.dot(down, hidden, preferred_element_type=F32)
    return resid.astype(F32) + update.astype(BF16).astype(F32)


def step_kernel(
    bands,
    state_ref,
    mask_ref,
    air_ref,
    temp_ref,
    flux_ref,
    ok_ref,
    ak_ref,
    ogain_ref,
    again_ref,
    fweight_ref,
    tweight_ref,
    oupraw_ref,
    odownraw_ref,
    aupraw_ref,
    adownraw_ref,
    onext_ref,
    anext_ref,
    stack,
    turned,
    cols_ref,
    oup_ref,
    odown_ref,
    aup_ref,
    otall,
    tl,
    fs,
    fl,
    es,
    er,
    ec,
    ew,
    ee,
    edge,
    ow,
    aw,
    oc,
    oo,
    ac,
    ao,
    owb,
    awb,
    omain,
    ototal,
    amain,
    awrap,
    atotal,
    send,
    recv,
    osend,
    orecv,
    asend,
    arecv,
):
    levels, band, och, lat = state_ref.shape
    alevels, halves, _, ach, part = air_ref.shape
    tiles = lat // LANES
    wide = band + 2 * RIM
    span = wide * 2 * RIM
    fields = fs.shape[0]
    last = band + RIM
    comp = lax.axis_index("comp")
    lon = lax.axis_index("lon")
    at = lax.axis_index("ch")
    count = 2 * bands
    place = comp * bands + lon
    west = lax.rem(place + count - 1, count)
    east = lax.rem(place + 1, count)
    o_west = {"comp": lax.div(west, bands), "lon": lax.rem(west, bands)}
    o_east = {"comp": lax.div(east, bands), "lon": lax.rem(east, bands)}
    a_west = {"lon": lax.rem(lon + bands - 1, bands)}
    a_east = {"lon": lax.rem(lon + 1, bands)}
    over = {"comp": 1 - comp}
    pair = {"ch": 1 - at}
    at_west = (lon == 0).astype(jnp.int32)
    at_east = (lon == bands - 1).astype(jnp.int32)

    barrier = pltpu.get_barrier_semaphore()
    for device in (over, pair, o_west, o_east, a_west, a_east):
        pl.semaphore_signal(barrier, inc=1, device_id=device, device_id_type=MESH)

    started = []

    def copy(src, dst, device):
        i = len(started)
        made = pltpu.make_async_remote_copy(
            src_ref=src,
            dst_ref=dst,
            send_sem=send.at[i],
            recv_sem=recv.at[i],
            device_id=device,
            device_id_type=MESH,
        )
        made.start()
        started.append(made)
        return made

    sea = mask_ref[...].astype(F32)
    own_temp = temp_ref[...] * sea
    for p in range(2):
        tl[comp, p] = own_temp[:, p * part : (p + 1) * part]
    for k in range(fields):
        low, high = flux_ref[k, :, 0, :], flux_ref[k, :, 1, :]
        fs[k] = jnp.where(comp == 0, high, low)
        fl[comp, k] = jnp.where(comp == 0, low, high)
    lane = lax.broadcasted_iota(jnp.int32, (ach, LANES), 1)

    def pack(tile, into, h, j, owner):
        base = (h * wide + RIM + j) * 2 * RIM
        begin = base + RIM * owner
        here = (lane >= begin) & (lane < begin + RIM)
        return jnp.where(here, pltpu.roll(tile, base + RIM, 1), into)

    for lev in range(1, levels):
        for j in range(band):
            v = state_ref[lev, j].astype(F32) * sea[j : j + 1, :]
            ow[lev, RIM + j] = v.astype(BF16)

    pl.semaphore_wait(barrier, 6)
    got_temp = copy(tl.at[comp], tl.at[comp], over)
    got_flux = copy(fs, fl.at[comp], over)
    deep = pl.ds(1, levels - 1)
    top = pl.ds(0, 1)
    first, final = pl.ds(RIM, RIM), pl.ds(last - RIM, RIM)
    low_rim, high_rim = pl.ds(0, RIM), pl.ds(last, RIM)
    ocean_rims = [
        copy(ow.at[deep, first], ow.at[deep, high_rim], o_west),
        copy(ow.at[deep, final], ow.at[deep, low_rim], o_east),
    ]

    for lev in range(alevels):
        packed = jnp.zeros((ach, LANES), F32)
        for h in range(halves):
            for j in range(band):
                packed = pack(air_ref[lev, h, j].astype(F32), packed, h, j, comp)
        es[lev] = packed.astype(BF16)
    got_edge = copy(es, er, over)

    stack[...] = jnp.zeros_like(stack)
    for at_row, ref in ((0, ogain_ref), (1, again_ref), (2, tweight_ref), (3, fweight_ref)):
        size = ref.shape[1]
        for begin in range(0, size, LANES):
            stop = min(begin + LANES, size)
            below = at_row + begin // LANES * HALF
            stack[below : below + ref.shape[0], 0 : stop - begin] = ref[:, begin:stop]
    flipped = jnp.transpose(stack[0:LANES, :])
    for block in range(cols_ref.shape[0] // LANES):
        cols_ref[block * LANES : (block + 1) * LANES, :] = flipped[
            :, block * HALF : (block + 1) * HALF
        ]
    spread_taps(ok_ref, stack, turned, owb)

    got_flux.wait_recv()
    for j in range(band):
        for p in range(tiles):
            inject = jnp.zeros((och, LANES), F32)
            for k in range(fields):
                inject += cols_ref[0:och, 3 + k : 4 + k] * fl[p, k, j : j + 1, :]
            cells = slice(p * LANES, (p + 1) * LANES)
            v = (state_ref[0, j, :, cells].astype(F32) + inject) * sea[j : j + 1, cells]
            ow[0, RIM + j, :, cells] = v.astype(BF16)
    ocean_rims.append(copy(ow.at[top, first], ow.at[top, high_rim], o_west))
    ocean_rims.append(copy(ow.at[top, final], ow.at[top, low_rim], o_east))

    got_temp.wait_recv()
    weight = cols_ref[0:ach, 2:3]
    for h in range(halves):
        for j in range(band):
            heat = weight * tl[h, comp, j : j + 1, :]
            aw[0, h, RIM + j] = (air_ref[0, h, j].astype(F32) + heat).astype(BF16)
            for lev in range(1, alevels):
                aw[lev, h, RIM + j] = air_ref[lev, h, j]
    air_rims = []
    every = pl.ds(0, alevels)
    for h in range(halves):
        to_west = lax.rem(h + (halves - 1) * at_west, halves)
        to_east = lax.rem(h + at_east, halves)
        air_rims.append(copy(aw.at[every, h, first], aw.at[every, to_west, high_rim], a_west))
        air_rims.append(copy(aw.at[every, h, final], aw.at[every, to_east, low_rim], a_east))
    got_edge.wait_recv()
    beyond = jnp.zeros((ach, LANES), F32)
    for h in range(halves):
        for j in range(band):
            row = jnp.broadcast_to(tl[h, 1 - comp, j : j + 1, :], (ach, LANES))
            beyond = pack(row, beyond, h, j, 1 - comp)
    ec[0] = (er[0].astype(F32) + weight * beyond).astype(BF16)
    for lev in range(1, alevels):
        ec[lev] = er[lev]
    edge_rims = [copy(ec, ee, a_west), copy(ec, ew, a_east)]

    spread_taps(ak_ref, stack, turned, awb)

    def swapped(ref):
        half = ref.shape[0] // 2
        mine = ref[pl.ds(pl.multiple_of(at * half, ROWS), half), :]
        other = ref[pl.ds(pl.multiple_of((1 - at) * half, ROWS), half), :]
        return jnp.concatenate([mine.astype(F32), other.astype(F32)], axis=0)

    oup_ref[...] = jnp.transpose(swapped(oupraw_ref)).astype(BF16)
    aup_ref[...] = jnp.transpose(swapped(aupraw_ref)).astype(BF16)
    otall[...] = jnp.transpose(odownraw_ref[...].astype(F32))
    odown_ref[...] = otall[pl.ds(pl.multiple_of(at * och, ROWS), och), :].astype(BF16)

    for made in ocean_rims:
        made.wait_recv()

    def ocean_copy(g):
        rows = pl.ds(pl.multiple_of(g * ROWS, ROWS), ROWS)
        return pltpu.make_async_remote_copy(
            src_ref=oc.at[:, :, rows, :],
            dst_ref=oo.at[:, :, rows, :],
            send_sem=osend.at[g],
            recv_sem=orecv.at[g],
            device_id=pair,
            device_id_type=MESH,
        )

    def ocean_body(g, carry):
        wider = pl.ds(pl.multiple_of(g * ROWS, ROWS), ROWS)
        for lev in range(levels):
            for p in range(tiles):
                cells = slice(p * LANES, (p + 1) * LANES)
                omain[lev, p] = ow[lev, :, wider, cells].astype(F32)

        def inner(sub, carry):
            rows = pl.ds(pl.multiple_of(sub * HALF, HALF), HALF)
            group = g * (ROWS // HALF) + sub
            ocean_group(omain, owb, ototal, rows, group, levels, tiles, band)
            return carry

        lax.fori_loop(0, ROWS // HALF, inner, 0)
        for lev in range(levels):
            for p in range(tiles):
                cells = slice(p * LANES, (p + 1) * LANES)
                oc[lev, :, wider, cells] = ototal[lev, p].astype(BF16)
        ocean_copy(g).start()
        return carry

    lax.fori_loop(0, och // ROWS, ocean_body, 0)

    for made in air_rims + edge_rims:
        made.wait_recv()
    step = band * 2 * RIM
    for lev in range(alevels):
        from_west, from_east = ew[lev].astype(F32), ee[lev].astype(F32)
        whole = ec[lev].astype(F32)
        for h in range(halves):
            west_h = lax.rem(h + (halves - 1) * at_west, halves)
            east_h = lax.rem(h + at_east, halves)
            shift = lax.rem((h - west_h) * span - step + 2 * LANES, LANES)
            here = (lane >= h * span) & (lane < h * span + 2 * RIM * RIM)
            whole = jnp.where(here, pltpu.roll(from_west, shift, 1), whole)
            shift = lax.rem((h - east_h) * span + step + 2 * LANES, LANES)
            here = (lane >= (h + 1) * span - 2 * RIM * RIM) & (lane < (h + 1) * span)
            whole = jnp.where(here, pltpu.roll(from_east, shift, 1), whole)
        edge[lev] = whole

    def air_copy(g):
        rows = pl.ds(pl.multiple_of(g * ROWS, ROWS), ROWS)
        return pltpu.make_async_remote_copy(
            src_ref=ac.at[:, :, :, rows, :],
            dst_ref=ao.at[:, :, :, rows, :],
            send_sem=asend.at[g],
            recv_sem=arecv.at[g],
            device_id=pair,
            device_id_type=MESH,
        )

    def air_body(g, carry):
        wider = pl.ds(pl.multiple_of(g * ROWS, ROWS), ROWS)
        for lev in range(alevels):
            for p in range(halves):
                amain[lev, p] = aw[lev, p, :, wider, :].astype(F32)

        def inner(sub, carry):
            rows = pl.ds(pl.multiple_of(sub * HALF, HALF), HALF)
            group = g * (ROWS // HALF) + sub
            these = pl.ds(pl.multiple_of(group * HALF, HALF), HALF)
            for lev in range(alevels):
                e = edge[lev, these, :]
                for p in range(halves):
                    for m in range(wide):
                        awrap[lev, p, m] = pltpu.roll(e, LANES - (p * wide + m) * 2 * RIM - RIM, 1)
            air_group(amain, awrap, awb, atotal, rows, group, alevels, halves, band)
            return carry

        lax.fori_loop(0, ROWS // HALF, inner, 0)
        for lev in range(alevels):
            for p in range(halves):
                ac[lev, p, :, wider, :] = atotal[lev, p].astype(BF16)
        air_copy(g).start()
        return carry

    lax.fori_loop(0, ach // ROWS, air_body, 0)

    def flat(cells):
        return jnp.concatenate([cells[j] for j in range(band)], axis=1)

    def ordered(column, ch):
        mine = cols_ref[pl.ds(pl.multiple_of(at * ch, HALF), ch), column : column + 1]
        other = cols_ref[pl.ds(pl.multiple_of((1 - at) * ch, HALF), ch), column : column + 1]
        return jnp.concatenate([mine, other], axis=0)

    lax.fori_loop(0, och // ROWS, lambda g, c: (ocean_copy(g).wait(), c)[1], 0)
    gain = ordered(0, och)

    def ocean_mlp(lev, carry):
        resid = flat(ow[lev, RIM : RIM + band])
        out = mlp(flat(oc[lev]), flat(oo[lev]), resid, gain, oup_ref[...], odown_ref[...])
        for j in range(band):
            v = out[:, j * lat : (j + 1) * lat] * mask_ref[j : j + 1, :].astype(F32)
            onext_ref[lev, j] = v.astype(BF16)
        return carry

    lax.fori_loop(0, levels, ocean_mlp, 0)
    lax.fori_loop(0, ach // ROWS, lambda g, c: (air_copy(g).wait(), c)[1], 0)
    again = ordered(1, ach)
    adown = adownraw_ref[pl.ds(pl.multiple_of(at * ach, ROWS), ach), :]

    def air_mlp(i, carry):
        lev, h = lax.div(i, halves), lax.rem(i, halves)
        resid = flat(aw[lev, h, RIM : RIM + band])
        out = mlp(flat(ac[lev, h]), flat(ao[lev, h]), resid, again, aup_ref[...], adown)
        for j in range(band):
            anext_ref[lev, h, j] = out[:, j * part : (j + 1) * part].astype(BF16)
        return carry

    lax.fori_loop(0, alevels * halves, air_mlp, 0)
    for made in started:
        made.wait_send()


def per_device(
    ocean_state,
    ocean_mask,
    air_state,
    surface_temp,
    air_fluxes,
    ocean_kernel,
    ocean_gain,
    ocean_up,
    ocean_down,
    air_kernel,
    air_gain,
    air_up,
    air_down,
    flux_weight,
    temp_weight,
):
    bands = lax.axis_size("lon")
    state = jnp.transpose(ocean_state, (0, 2, 1, 3))
    air = jnp.transpose(air_state, (0, 3, 2, 1, 4))
    levels, band, och, lat = state.shape
    alevels, halves, _, ach, part = air.shape
    fields = air_fluxes.shape[0]
    wide = band + 2 * RIM
    tiles = lat // LANES
    height = -(-max(ocean_gain.shape[0], air_gain.shape[0]) // LANES) * LANES
    ohid, ahid = ocean_up.shape[1], air_up.shape[1]
    edge = (alevels, ach, LANES)
    scratch = [
        pltpu.VMEM((2 * LANES, LANES), F32),
        pltpu.VMEM((2, LANES, LANES), F32),
        pltpu.VMEM((height, HALF), F32),
        pltpu.VMEM((ohid, 2 * och), BF16),
        pltpu.VMEM((och, ohid), BF16),
        pltpu.VMEM((ahid, 2 * ach), BF16),
        pltpu.VMEM((2 * och, ohid), F32),
        pltpu.VMEM((halves, 2, band, part), F32),
        pltpu.VMEM((fields, band, part), F32),
        pltpu.VMEM((2, fields, band, part), F32),
        pltpu.VMEM(edge, BF16),
        pltpu.VMEM(edge, BF16),
        pltpu.VMEM(edge, BF16),
        pltpu.VMEM(edge, BF16),
        pltpu.VMEM(edge, BF16),
        pltpu.VMEM(edge, F32),
        pltpu.VMEM((levels, wide, och, lat), BF16),
        pltpu.VMEM((alevels, halves, wide, ach, part), BF16),
        pltpu.VMEM(state.shape, BF16),
        pltpu.VMEM(state.shape, BF16),
        pltpu.VMEM(air.shape, BF16),
        pltpu.VMEM(air.shape, BF16),
        pltpu.VMEM((och // HALF, TAPS, HALF, LANES), F32),
        pltpu.VMEM((ach // HALF, TAPS, HALF, LANES), F32),
        pltpu.VMEM((levels, tiles, wide, ROWS, LANES), F32),
        pltpu.VMEM((levels, tiles, band, ROWS, LANES), F32),
        pltpu.VMEM((alevels, halves, wide, ROWS, LANES), F32),
        pltpu.VMEM((alevels, halves, wide, HALF, LANES), F32),
        pltpu.VMEM((alevels, halves, band, ROWS, LANES), F32),
        pltpu.SemaphoreType.DMA((9 + 2 * halves,)),
        pltpu.SemaphoreType.DMA((9 + 2 * halves,)),
        pltpu.SemaphoreType.DMA((och // ROWS,)),
        pltpu.SemaphoreType.DMA((och // ROWS,)),
        pltpu.SemaphoreType.DMA((ach // ROWS,)),
        pltpu.SemaphoreType.DMA((ach // ROWS,)),
    ]
    vmem = pl.BlockSpec(memory_space=pltpu.VMEM)
    ocean_next, air_next = pl.pallas_call(
        functools.partial(step_kernel, bands),
        out_shape=(
            jax.ShapeDtypeStruct(state.shape, BF16),
            jax.ShapeDtypeStruct(air.shape, BF16),
        ),
        in_specs=[vmem] * 15,
        out_specs=(vmem, vmem),
        scratch_shapes=scratch,
        compiler_params=pltpu.CompilerParams(
            collective_id=0, has_side_effects=True, vmem_limit_bytes=52 * 1024 * 1024
        ),
        cost_estimate=pl.CostEstimate(
            flops=2_000_000_000, bytes_accessed=4_000_000, transcendentals=3_000_000
        ),
    )(
        state,
        ocean_mask,
        air,
        surface_temp,
        air_fluxes,
        jnp.transpose(ocean_kernel, (1, 2, 3, 0)),
        jnp.transpose(air_kernel, (1, 2, 3, 0)),
        ocean_gain[None],
        air_gain[None],
        flux_weight,
        temp_weight[None],
        ocean_up,
        ocean_down,
        air_up,
        air_down.T,
    )
    return jnp.transpose(ocean_next, (0, 2, 1, 3)), jnp.transpose(air_next, (0, 3, 2, 1, 4))


def solution(mesh):
    in_specs = (
        P(None, "ch", ("comp", "lon"), None),
        P(("comp", "lon"), None),
        P(None, "ch", "lon", None, "comp"),
        P(("comp", "lon"), None),
        P(None, "lon", None, "comp"),
        P("ch", None, None, None),
        P(),
        P(),
        P(),
        P("ch", None, None, None),
        P(),
        P(),
        P(),
        P(None, "ch"),
        P("ch"),
    )
    out_specs = (P(None, "ch", ("comp", "lon"), None), P(None, "ch", "lon", None, "comp"))
    return jax.shard_map(
        per_device, mesh=mesh, in_specs=in_specs, out_specs=out_specs, check_vma=False
    )
```

profile of v0, /device:TPU:0, one launch (start us, length us, event | category | flops | bytes accessed | tf_op | source)
XLA Modules:
  0.0 45.4 jit_solution(6234376966229705179)
XLA Ops:
  0.6 0.0 copy-start.13
  0.6 0.0 copy-start.3
  0.7 0.0 copy-start.4
  0.7 0.0 copy-start.5
  0.7 1.9 %copy.24 = bf16[3,64,4,256]{3,1,2,0:T(8,128)(2,1)} copy(bf16[3,64,4,256]{3,2,1,0:T(4,128)(2,1)} %param.15) | data formatting | bytes 786432 | tf_op args[0]
  2.5 0.0 copy-done.13
  2.5 0.0 copy-start
  2.5 0.0 copy-start.1
  2.5 0.0 copy-start.2
  2.5 0.0 copy-start.6
  2.5 0.0 copy-start.7
  2.6 0.0 copy-start.8
  2.6 0.0 copy-start.9
  2.6 0.0 copy-start.12
  2.6 0.8 %copy.23 = bf16[2,96,4,2,128]{4,1,2,3,0:T(8,128)(2,1)} copy(bf16[2,96,4,2,128]{4,3,2,1,0:T(2,128)(2,1)S(1)} %copy-done.13) | data formatting | bytes 786432 | tf_op args[2]
  3.4 0.0 copy-start.10
  3.4 0.0 copy-start.11
  3.4 0.0 copy-done.3
  3.4 0.0 copy-done.4
  3.4 0.0 copy-done.5
  3.4 0.1 copy-done
  3.5 0.2 copy-done.1
  3.7 0.1 copy-done.2
  3.7 0.0 copy-done.6
  3.8 0.0 copy-done.7
  3.8 0.0 copy-done.8
  3.8 0.0 copy-done.9
  3.8 0.0 copy-done.12
  3.8 0.4 copy-done.10
  4.1 0.0 copy-done.11
  4.1 39.0 %shard_map.158 = (bf16[3,4,64,256]{3,2,1,0:T(8,128)(2,1)S(1)}, bf16[2,2,4,96,128]{4,3,2,1,0:T(8,128)(2,1)S(1)}) custom-call(bf16[3,4,64,256]{3,2,1,0:T(8,128)(2,1)} %bitcast.22, s32[4,256]{1,0:T(4,128)S(1)} %copy-done.7, bf16[2,2,4,96,128]{4,3,2,1,0:T(8,128)(2,1)} %bitcast.23, f32[4,256]{1,0:T(4,128)S(1)} %copy-done.8, f32[4,4,2,128]{3,2,1,0:T(2,128)S(1)} %copy-done.6, ...), custom_call_target="tpu_custom_call" | custom-call | flops 2000000000 | bytes 4000000 | tf_op jit(solution)/shard_map/pallas_call | solution.py:513
  43.2 1.1 %copy.19 = bf16[3,64,4,256]{3,2,1,0:T(4,128)(2,1)} copy(bf16[3,64,4,256]{3,1,2,0:T(8,128)(2,1)S(1)} %bitcast.15) | data formatting | bytes 786432
  44.2 1.1 %copy.20 = bf16[2,96,4,2,128]{4,3,2,1,0:T(2,128)(2,1)} copy(bf16[2,96,4,2,128]{4,1,2,3,0:T(8,128)(2,1)S(1)} %bitcast.14) | data formatting | bytes 786432
Async XLA Ops:
  0.6 1.9 %copy-start.13 = (bf16[2,96,4,2,128]{4,3,2,1,0:T(2,128)(2,1)S(1)}, bf16[2,96,4,2,128]{4,3,2,1,0:T(2,128)(2,1)}, u32[]{:S(2)}) copy-start(bf16[2,96,4,2,128]{4,3,2,1,0:T(2,128)(2,1)} %param.17) | copy-start | bytes 1179652
  0.6 2.8 %copy-start.3 = (bf16[512,128]{1,0:T(8,128)(2,1)S(1)}, bf16[512,128]{1,0:T(8,128)(2,1)}, u32[]{:S(2)}) copy-start(bf16[512,128]{1,0:T(8,128)(2,1)} %odownraw_ref.1) | copy-start | bytes 393220
  0.7 2.8 %copy-start.4 = (f32[64,3,7,7]{0,3,2,1:T(8,128)S(1)}, f32[64,3,7,7]{0,3,2,1:T(8,128)}, u32[]{:S(2)}) copy-start(f32[64,3,7,7]{0,3,2,1:T(8,128)} %param.20) | copy-start | bytes 112900
  0.7 2.8 %copy-start.5 = (f32[96,3,7,7]{0,3,2,1:T(8,128)S(1)}, f32[96,3,7,7]{0,3,2,1:T(8,128)}, u32[]{:S(2)}) copy-start(f32[96,3,7,7]{0,3,2,1:T(8,128)} %param.24) | copy-start | bytes 169348
  2.5 1.0 %copy-start = (bf16[192,768]{1,0:T(8,128)(2,1)S(1)}, bf16[192,768]{1,0:T(8,128)(2,1)}, u32[]{:S(2)}) copy-start(bf16[192,768]{1,0:T(8,128)(2,1)} %aupraw_ref.1) | copy-start | bytes 884740
  2.5 1.1 %copy-start.1 = (bf16[768,192]{0,1:T(8,128)(2,1)S(1)}, bf16[768,192]{0,1:T(8,128)(2,1)}, u32[]{:S(2)}) copy-start(bf16[768,192]{0,1:T(8,128)(2,1)} %param.27) | copy-start | bytes 884740
  2.5 1.2 %copy-start.2 = (bf16[128,512]{1,0:T(8,128)(2,1)S(1)}, bf16[128,512]{1,0:T(8,128)(2,1)}, u32[]{:S(2)}) copy-start(bf16[128,512]{1,0:T(8,128)(2,1)} %oupraw_ref.1) | copy-start | bytes 393220
  2.5 1.2 %copy-start.6 = (f32[4,4,2,128]{3,2,1,0:T(2,128)S(1)}, f32[4,4,2,128]{3,2,1,0:T(2,128)}, u32[]{:S(2)}) copy-start(f32[4,4,2,128]{3,2,1,0:T(2,128)} %flux_ref.1) | copy-start | bytes 49156
  2.5 1.2 %copy-start.7 = (s32[4,256]{1,0:T(4,128)S(1)}, s32[4,256]{1,0:T(4,128)}, u32[]{:S(2)}) copy-start(s32[4,256]{1,0:T(4,128)} %mask_ref.1) | copy-start | bytes 12292
  2.6 1.2 %copy-start.8 = (f32[4,256]{1,0:T(4,128)S(1)}, f32[4,256]{1,0:T(4,128)}, u32[]{:S(2)}) copy-start(f32[4,256]{1,0:T(4,128)} %temp_ref.1) | copy-start | bytes 12292
  2.6 1.2 %copy-start.9 = (f32[4,64]{1,0:T(4,128)S(1)}, f32[4,64]{1,0:T(4,128)}, u32[]{:S(2)}) copy-start(f32[4,64]{1,0:T(4,128)} %fweight_ref.1) | copy-start | bytes 3076
  2.6 1.2 %copy-start.12 = (f32[96]{0:T(128)S(1)}, f32[96]{0:T(128)}, u32[]{:S(2)}) copy-start(f32[96]{0:T(128)} %param.29) | copy-start | bytes 1156
  3.4 0.7 %copy-start.10 = (f32[192]{0:T(256)S(1)}, f32[192]{0:T(256)}, u32[]{:S(2)}) copy-start(f32[192]{0:T(256)} %param.25) | copy-start | bytes 2308
  3.4 0.7 %copy-start.11 = (f32[128]{0:T(128)S(1)}, f32[128]{0:T(128)}, u32[]{:S(2)}) copy-start(f32[128]{0:T(128)} %param.21) | copy-start | bytes 1540
where the time goes:
time: 45.6 us; the launch traced here: 45.4 us
  Pallas kernels  39 us (86%)
  local copies, waits for them, and re-layouts  5.6 us (12%)
  between operations  0.75 us (2%)
    pallas_call x1, Pallas kernels, per_device(): pl.pallas_call(functools.partial(step_kernel, bands), out_shape=(jax.Shap...  39 us
    unnamed x32, local copies, waits for them, and re-layouts  5.6 us

commit v1 on v0

--- a/solution.py
+++ b/solution.py
@@ -53,25 +53,44 @@
                     total[lev, p, :, rows, :] += v
 
 
-def air_group(main, wrap, wb, total, rows, group, levels, halves, width):
-    lane = lax.broadcasted_iota(jnp.int32, (width + 2 * RIM, HALF, LANES), 2)
+def air_group(main, edge, slot, wb, total, rows, group, levels, halves, width):
+    lane = lax.broadcasted_iota(jnp.int32, (width, HALF, LANES), 2)
+    pair = 2 * RIM
+    turned = [
+        [pltpu.roll(e, LANES - pair * b, 2) if b else e for b in range(7)] for e in edge
+    ]
+    rim = [jnp.zeros((1, HALF, LANES), F32) for _ in range(levels)]
+    for d in (0, 1, 2, 4, 5, 6):
+        sums = tap_sum(lambda lev, b: turned[lev][b], wb, group, d, levels, 1)
+        if d < RIM:
+            move, here = LANES - d, (slot >= RIM) & (slot < pair - d)
+        else:
+            move, here = 6 - d, (slot < RIM) & (slot >= 6 - d)
+        for lev in range(levels):
+            v = pltpu.roll(sums[lev], move, 2) if move % LANES else sums[lev]
+            rim[lev] += jnp.where(here, v, 0.0)
+    ends = (lane < RIM) | (lane >= LANES - RIM)
     for p in range(halves):
         for step, d in enumerate((3, 0, 1, 2, 4, 5, 6)):
             s = d - 3
-            shifted = []
+            sums = tap_sum(
+                lambda lev, b: main[lev, p, b : b + width, rows, :], wb, group, d, levels, width
+            )
             for lev in range(levels):
-                v = main[lev, p, :, rows, :]
+                v = sums[lev]
                 if s > 0:
-                    v = pltpu.roll(jnp.where(lane < s, wrap[lev, p], v), LANES - s, 2)
+                    v = pltpu.roll(jnp.where(lane < s, 0.0, v), LANES - s, 2)
                 elif s < 0:
-                    v = pltpu.roll(jnp.where(lane >= LANES + s, wrap[lev, p], v), -s, 2)
-                shifted.append(v)
-            sums = tap_sum(lambda lev, b: shifted[lev][b : b + width], wb, group, d, levels, width)
-            for lev in range(levels):
+                    v = pltpu.roll(jnp.where(lane >= LANES + s, 0.0, v), -s, 2)
                 if step == 0:
-                    total[lev, p, :, rows, :] = sums[lev]
+                    begin = p * (width + pair) * pair + RIM
+                    tips = [
+                        pltpu.roll(rim[lev], LANES - begin - j * pair, 2) for j in range(width)
+                    ]
+                    v += jnp.where(ends, jnp.concatenate(tips, axis=0), 0.0)
+                    total[lev, p, :, rows, :] = v
                 else:
-                    total[lev, p, :, rows, :] += sums[lev]
+                    total[lev, p, :, rows, :] += v
 
 
 def spread_taps(k_ref, stack, turned, wb):
@@ -157,7 +176,7 @@
     omain,
     ototal,
     amain,
-    awrap,
+    slot_ref,
     atotal,
     send,
     recv,
@@ -221,9 +240,9 @@
 
     def pack(tile, into, h, j, owner):
         base = (h * wide + RIM + j) * 2 * RIM
-        begin = base + RIM * owner
+        begin = base + RIM * (1 - owner)
         here = (lane >= begin) & (lane < begin + RIM)
-        return jnp.where(here, pltpu.roll(tile, base + RIM, 1), into)
+        return jnp.where(here, pltpu.roll(tile, base + 2 * RIM * (1 - owner), 1), into)
 
     for lev in range(1, levels):
         for j in range(band):
@@ -284,13 +303,6 @@
             aw[0, h, RIM + j] = (air_ref[0, h, j].astype(F32) + heat).astype(BF16)
             for lev in range(1, alevels):
                 aw[lev, h, RIM + j] = air_ref[lev, h, j]
-    air_rims = []
-    every = pl.ds(0, alevels)
-    for h in range(halves):
-        to_west = lax.rem(h + (halves - 1) * at_west, halves)
-        to_east = lax.rem(h + at_east, halves)
-        air_rims.append(copy(aw.at[every, h, first], aw.at[every, to_west, high_rim], a_west))
-        air_rims.append(copy(aw.at[every, h, final], aw.at[every, to_east, low_rim], a_east))
     got_edge.wait_recv()
     beyond = jnp.zeros((ach, LANES), F32)
     for h in range(halves):
@@ -300,7 +312,6 @@
     ec[0] = (er[0].astype(F32) + weight * beyond).astype(BF16)
     for lev in range(1, alevels):
         ec[lev] = er[lev]
-    edge_rims = [copy(ec, ee, a_west), copy(ec, ew, a_east)]
 
     spread_taps(ak_ref, stack, turned, awb)
 
@@ -315,8 +326,19 @@
     otall[...] = jnp.transpose(odownraw_ref[...].astype(F32))
     odown_ref[...] = otall[pl.ds(pl.multiple_of(at * och, ROWS), och), :].astype(BF16)
 
+    slot_ref[...] = lax.rem(
+        lax.broadcasted_iota(jnp.int32, (1, HALF, LANES), 2), jnp.int32(2 * RIM)
+    )
     for made in ocean_rims:
         made.wait_recv()
+    edge_rims = [copy(ec, ee, a_west), copy(ec, ew, a_east)]
+    air_rims = []
+    every = pl.ds(0, alevels)
+    for h in range(halves):
+        to_west = lax.rem(h + (halves - 1) * at_west, halves)
+        to_east = lax.rem(h + at_east, halves)
+        air_rims.append(copy(aw.at[every, h, first], aw.at[every, to_west, high_rim], a_west))
+        air_rims.append(copy(aw.at[every, h, final], aw.at[every, to_east, low_rim], a_east))
 
     def ocean_copy(g):
         rows = pl.ds(pl.multiple_of(g * ROWS, ROWS), ROWS)
@@ -390,12 +412,8 @@
             rows = pl.ds(pl.multiple_of(sub * HALF, HALF), HALF)
             group = g * (ROWS // HALF) + sub
             these = pl.ds(pl.multiple_of(group * HALF, HALF), HALF)
-            for lev in range(alevels):
-                e = edge[lev, these, :]
-                for p in range(halves):
-                    for m in range(wide):
-                        awrap[lev, p, m] = pltpu.roll(e, LANES - (p * wide + m) * 2 * RIM - RIM, 1)
-            air_group(amain, awrap, awb, atotal, rows, group, alevels, halves, band)
+            ends = [edge[lev, these, :][None] for lev in range(alevels)]
+            air_group(amain, ends, slot_ref[...], awb, atotal, rows, group, alevels, halves, band)
             return carry
 
         lax.fori_loop(0, ROWS // HALF, inner, 0)
@@ -500,7 +518,7 @@
         pltpu.VMEM((levels, tiles, wide, ROWS, LANES), F32),
         pltpu.VMEM((levels, tiles, band, ROWS, LANES), F32),
         pltpu.VMEM((alevels, halves, wide, ROWS, LANES), F32),
-        pltpu.VMEM((alevels, halves, wide, HALF, LANES), F32),
+        pltpu.VMEM((1, HALF, LANES), jnp.int32),
         pltpu.VMEM((alevels, halves, band, ROWS, LANES), F32),
         pltpu.SemaphoreType.DMA((9 + 2 * halves,)),
         pltpu.SemaphoreType.DMA((9 + 2 * halves,)),

time: 45.6 us -> 45.6 us (level)
  no operation moved by 1% of the time
where the time goes in v1:
time: 45.6 us; the launch traced here: 45.4 us
  Pallas kernels  39 us (86%)
  local copies, waits for them, and re-layouts  5.6 us (12%)
  between operations  0.75 us (2%)
    pallas_call x1, Pallas kernels, per_device(): pl.pallas_call(functools.partial(step_kernel, bands), out_shape=(jax.Shap...  39 us
    unnamed x32, local copies, waits for them, and re-layouts  5.6 us

profile of v1, /device:TPU:0, one launch (start us, length us, event | category | flops | bytes accessed | tf_op | source)
XLA Modules:
  0.0 45.4 jit_solution(10800948653000843519)
XLA Ops:
  0.6 0.0 copy-start.13
  0.6 0.0 copy-start.3
  0.7 0.0 copy-start.4
  0.7 0.0 copy-start.5
  0.7 1.9 %copy.24 = bf16[3,64,4,256]{3,1,2,0:T(8,128)(2,1)} copy(bf16[3,64,4,256]{3,2,1,0:T(4,128)(2,1)} %param.15) | data formatting | bytes 786432 | tf_op args[0]
  2.5 0.0 copy-done.13
  2.5 0.0 copy-start
  2.5 0.0 copy-start.1
  2.5 0.0 copy-start.2
  2.5 0.0 copy-start.6
  2.5 0.0 copy-start.7
  2.6 0.0 copy-start.8
  2.6 0.0 copy-start.9
  2.6 0.0 copy-start.12
  2.6 0.8 %copy.23 = bf16[2,96,4,2,128]{4,1,2,3,0:T(8,128)(2,1)} copy(bf16[2,96,4,2,128]{4,3,2,1,0:T(2,128)(2,1)S(1)} %copy-done.13) | data formatting | bytes 786432 | tf_op args[2]
  3.4 0.0 copy-start.10
  3.4 0.0 copy-start.11
  3.4 0.0 copy-done.3
  3.4 0.0 copy-done.4
  3.4 0.0 copy-done.5
  3.4 0.1 copy-done
  3.5 0.2 copy-done.1
  3.7 0.1 copy-done.2
  3.7 0.0 copy-done.6
  3.8 0.0 copy-done.7
  3.8 0.0 copy-done.8
  3.8 0.0 copy-done.9
  3.8 0.0 copy-done.12
  3.8 0.4 copy-done.10
  4.1 0.0 copy-done.11
  4.1 39.0 %shard_map.158 = (bf16[3,4,64,256]{3,2,1,0:T(8,128)(2,1)S(1)}, bf16[2,2,4,96,128]{4,3,2,1,0:T(8,128)(2,1)S(1)}) custom-call(bf16[3,4,64,256]{3,2,1,0:T(8,128)(2,1)} %bitcast.22, s32[4,256]{1,0:T(4,128)S(1)} %copy-done.7, bf16[2,2,4,96,128]{4,3,2,1,0:T(8,128)(2,1)} %bitcast.23, f32[4,256]{1,0:T(4,128)S(1)} %copy-done.8, f32[4,4,2,128]{3,2,1,0:T(2,128)S(1)} %copy-done.6, ...), custom_call_target="tpu_custom_call" | custom-call | flops 2000000000 | bytes 4000000 | tf_op jit(solution)/shard_map/pallas_call | solution.py:531
  43.2 1.1 %copy.19 = bf16[3,64,4,256]{3,2,1,0:T(4,128)(2,1)} copy(bf16[3,64,4,256]{3,1,2,0:T(8,128)(2,1)S(1)} %bitcast.15) | data formatting | bytes 786432
  44.2 1.1 %copy.20 = bf16[2,96,4,2,128]{4,3,2,1,0:T(2,128)(2,1)} copy(bf16[2,96,4,2,128]{4,1,2,3,0:T(8,128)(2,1)S(1)} %bitcast.14) | data formatting | bytes 786432
Async XLA Ops:
  0.6 1.9 %copy-start.13 = (bf16[2,96,4,2,128]{4,3,2,1,0:T(2,128)(2,1)S(1)}, bf16[2,96,4,2,128]{4,3,2,1,0:T(2,128)(2,1)}, u32[]{:S(2)}) copy-start(bf16[2,96,4,2,128]{4,3,2,1,0:T(2,128)(2,1)} %param.17) | copy-start | bytes 1179652
  0.6 2.8 %copy-start.3 = (bf16[512,128]{1,0:T(8,128)(2,1)S(1)}, bf16[512,128]{1,0:T(8,128)(2,1)}, u32[]{:S(2)}) copy-start(bf16[512,128]{1,0:T(8,128)(2,1)} %odownraw_ref.1) | copy-start | bytes 393220
  0.7 2.8 %copy-start.4 = (f32[64,3,7,7]{0,3,2,1:T(8,128)S(1)}, f32[64,3,7,7]{0,3,2,1:T(8,128)}, u32[]{:S(2)}) copy-start(f32[64,3,7,7]{0,3,2,1:T(8,128)} %param.20) | copy-start | bytes 112900
  0.7 2.8 %copy-start.5 = (f32[96,3,7,7]{0,3,2,1:T(8,128)S(1)}, f32[96,3,7,7]{0,3,2,1:T(8,128)}, u32[]{:S(2)}) copy-start(f32[96,3,7,7]{0,3,2,1:T(8,128)} %param.24) | copy-start | bytes 169348
  2.5 1.0 %copy-start = (bf16[192,768]{1,0:T(8,128)(2,1)S(1)}, bf16[192,768]{1,0:T(8,128)(2,1)}, u32[]{:S(2)}) copy-start(bf16[192,768]{1,0:T(8,128)(2,1)} %aupraw_ref.1) | copy-start | bytes 884740
  2.5 1.1 %copy-start.1 = (bf16[768,192]{0,1:T(8,128)(2,1)S(1)}, bf16[768,192]{0,1:T(8,128)(2,1)}, u32[]{:S(2)}) copy-start(bf16[768,192]{0,1:T(8,128)(2,1)} %param.27) | copy-start | bytes 884740
  2.5 1.2 %copy-start.2 = (bf16[128,512]{1,0:T(8,128)(2,1)S(1)}, bf16[128,512]{1,0:T(8,128)(2,1)}, u32[]{:S(2)}) copy-start(bf16[128,512]{1,0:T(8,128)(2,1)} %oupraw_ref.1) | copy-start | bytes 393220
  2.5 1.2 %copy-start.6 = (f32[4,4,2,128]{3,2,1,0:T(2,128)S(1)}, f32[4,4,2,128]{3,2,1,0:T(2,128)}, u32[]{:S(2)}) copy-start(f32[4,4,2,128]{3,2,1,0:T(2,128)} %flux_ref.1) | copy-start | bytes 49156
  2.5 1.2 %copy-start.7 = (s32[4,256]{1,0:T(4,128)S(1)}, s32[4,256]{1,0:T(4,128)}, u32[]{:S(2)}) copy-start(s32[4,256]{1,0:T(4,128)} %mask_ref.1) | copy-start | bytes 12292
  2.6 1.2 %copy-start.8 = (f32[4,256]{1,0:T(4,128)S(1)}, f32[4,256]{1,0:T(4,128)}, u32[]{:S(2)}) copy-start(f32[4,256]{1,0:T(4,128)} %temp_ref.1) | copy-start | bytes 12292
  2.6 1.2 %copy-start.9 = (f32[4,64]{1,0:T(4,128)S(1)}, f32[4,64]{1,0:T(4,128)}, u32[]{:S(2)}) copy-start(f32[4,64]{1,0:T(4,128)} %fweight_ref.1) | copy-start | bytes 3076
  2.6 1.2 %copy-start.12 = (f32[96]{0:T(128)S(1)}, f32[96]{0:T(128)}, u32[]{:S(2)}) copy-start(f32[96]{0:T(128)} %param.29) | copy-start | bytes 1156
  3.4 0.7 %copy-start.10 = (f32[192]{0:T(256)S(1)}, f32[192]{0:T(256)}, u32[]{:S(2)}) copy-start(f32[192]{0:T(256)} %param.25) | copy-start | bytes 2308
  3.4 0.7 %copy-start.11 = (f32[128]{0:T(128)S(1)}, f32[128]{0:T(128)}, u32[]{:S(2)}) copy-start(f32[128]{0:T(128)} %param.21) | copy-start | bytes 1540
